TPU v7x, 512 devices: a whole 4x8x8 slice. The times are simulated.
512 devices in a mesh: expert: 32 (over y_hi, z), dp: 16 (over x, y_lo, core).
Axes of the slice: x: 4, y: 8 (y_hi: 4, y_lo: 2; y = y_hi * 2 + y_lo), z: 8, core: 2. Of those that a mesh axis runs over, the one named last changes fastest.
Arguments:
- tokens: bfloat16 [65536, 2560], P(('expert', 'dp')), may hold values from -6 to 6
- cotangent: bfloat16 [65536, 2560], P(('expert', 'dp')), may hold values from -6 to 6
- gates: bfloat16 [65536, 2], P(('expert', 'dp')), may hold values from 0.099609375 to 1
- routes: int32 [65536, 2], P(('expert', 'dp')), may hold values from -1 to 7, as said below
- gate_proj: bfloat16 [32, 192, 2560], P('expert', 'dp'), may hold values from -0.125 to 0.125
- up_proj: bfloat16 [32, 192, 2560], P('expert', 'dp'), may hold values from -0.125 to 0.125
- down_proj: bfloat16 [32, 192, 2560], P('expert', 'dp'), may hold values from -0.21875 to 0.21875
Outputs:
- grad_tokens: bfloat16 [65536, 2560], P(('expert', 'dp'))
- grad_gates: float32 [65536, 2], P(('expert', 'dp'))
- grad_gate_proj: bfloat16 [32, 192, 2560], P('expert', 'dp')
- grad_up_proj: bfloat16 [32, 192, 2560], P('expert', 'dp')
- grad_down_proj: bfloat16 [32, 192, 2560], P('expert', 'dp')
Inputs may be any that keep to these rules, and one draw needn't show every extreme that they name: `routes`: each row lists 1 to 2 different experts in its first entries and -1 in the others.
All inputs are finite; a program needn't handle non-finite values.
Results may differ from a plain program's by a relative error of at most 0.0085.
Values may be sent and summed in bfloat16 or wider, within the bound.
A program may use at most 64 MiB of HBM per device.

v0:
```python
import jax
import jax.numpy as jnp
from jax import lax
from jax.sharding import PartitionSpec as P

GROUP = 4


def slot_tables(route_block, experts, capacity):
    expert_range = jnp.arange(experts, dtype=jnp.int32)
    named = route_block[:, :, None] == expert_range[None, None, :]
    hits = jnp.sum(named.astype(jnp.int32), axis=1)
    before = jnp.cumsum(hits, axis=0) - hits
    rank_pick = jnp.sum(jnp.where(named, before[:, None, :], 0), axis=2)
    kept_slot = (route_block >= 0) & (rank_pick < capacity)
    slot_ids = jnp.where(kept_slot, route_block * capacity + rank_pick, -1)
    return slot_ids


def unit_pass(rows_x, scaled_dy, gate_rows, up_rows, down_rows):
    contract = (((1,), (1,)), ((), ()))
    pre_gate = lax.dot_general(rows_x, gate_rows, contract, preferred_element_type=jnp.float32)
    pre_up = lax.dot_general(rows_x, up_rows, contract, preferred_element_type=jnp.float32)
    sigmoid_gate = jax.nn.sigmoid(pre_gate)
    activated = pre_gate * sigmoid_gate
    hidden = (activated * pre_up).astype(jnp.bfloat16)
    outward = jnp.dot(hidden, down_rows, preferred_element_type=jnp.float32)
    grad_hidden = lax.dot_general(
        scaled_dy, down_rows, contract, preferred_element_type=jnp.float32
    )
    grad_pre_gate = (
        grad_hidden * pre_up * sigmoid_gate * (1.0 + pre_gate * (1.0 - sigmoid_gate))
    ).astype(jnp.bfloat16)
    grad_pre_up = (grad_hidden * activated).astype(jnp.bfloat16)
    slot_grad = jnp.dot(grad_pre_gate, gate_rows, preferred_element_type=jnp.float32) + jnp.dot(
        grad_pre_up, up_rows, preferred_element_type=jnp.float32
    )
    return (hidden, grad_pre_gate, grad_pre_up, outward, slot_grad)


def spread_out(buffer, experts, capacity):
    shaped = buffer.reshape((experts, 1, capacity) + buffer.shape[1:])
    copies = jnp.broadcast_to(shaped, (experts, GROUP, capacity) + buffer.shape[1:])
    return copies.reshape((experts * GROUP, capacity) + buffer.shape[1:])


def per_device(tokens, cotangent, gates, routes, gate_proj, up_proj, down_proj):
    tok_rows, model_width = tokens.shape
    members = lax.axis_size("expert")
    experts = members // GROUP
    capacity = max(2, tok_rows // experts)
    slot_count = experts * capacity
    slot_ids = slot_tables(routes, experts, capacity)
    slot_range = jnp.arange(slot_count, dtype=jnp.int32)
    picked = slot_ids[None, :, :] == slot_range[:, None, None]
    placing = jnp.any(picked, axis=2)
    place_bf = placing.astype(jnp.bfloat16)
    sent_x = jnp.dot(place_bf, tokens, preferred_element_type=jnp.float32).astype(jnp.bfloat16)
    sent_dy = jnp.dot(place_bf, cotangent, preferred_element_type=jnp.float32).astype(jnp.bfloat16)
    sent_gate = jnp.sum(
        jnp.where(picked, gates.astype(jnp.float32)[None, :, :], 0.0), axis=(1, 2)
    ).astype(jnp.bfloat16)
    got_x, got_dy, got_gate = (
        lax.all_to_all(
            spread_out(sent_x, experts, capacity), "expert", split_axis=0, concat_axis=0, tiled=True
        ),
        lax.all_to_all(
            spread_out(sent_dy, experts, capacity),
            "expert",
            split_axis=0,
            concat_axis=0,
            tiled=True,
        ),
        lax.all_to_all(
            spread_out(sent_gate, experts, capacity),
            "expert",
            split_axis=0,
            concat_axis=0,
            tiled=True,
        ),
    )
    rows_x = got_x.reshape(-1, model_width)
    rows_dy = got_dy.reshape(-1, model_width)
    rows_gate = got_gate.reshape(-1).astype(jnp.float32)
    scaled_dy = (rows_gate[:, None] * rows_dy.astype(jnp.float32)).astype(jnp.bfloat16)
    full_gate, full_up, full_down = (
        lax.all_gather(gate_proj, "dp", axis=1, tiled=True),
        lax.all_gather(up_proj, "dp", axis=1, tiled=True),
        lax.all_gather(down_proj, "dp", axis=1, tiled=True),
    )
    hidden, grad_pre_gate, grad_pre_up, outward, slot_grad = unit_pass(
        rows_x, scaled_dy, full_gate[0], full_up[0], full_down[0]
    )
    gate_part = jnp.sum(rows_dy.astype(jnp.float32) * outward, axis=1).astype(jnp.bfloat16)
    slot_part = slot_grad.astype(jnp.bfloat16)
    contract_rows = (((0,), (0,)), ((), ()))
    term_gate = lax.dot_general(
        grad_pre_gate, rows_x, contract_rows, preferred_element_type=jnp.float32
    )
    term_up = lax.dot_general(
        grad_pre_up, rows_x, contract_rows, preferred_element_type=jnp.float32
    )
    term_down = lax.dot_general(
        hidden, scaled_dy, contract_rows, preferred_element_type=jnp.float32
    )
    whole_term = jnp.stack([term_gate, term_up, term_down], axis=1).astype(jnp.bfloat16)
    parted = whole_term.reshape(lax.axis_size("dp"), gate_proj.shape[1], 3, model_width)
    swapped = lax.all_to_all(parted, "dp", split_axis=0, concat_axis=0, tiled=True)
    shares = jnp.sum(swapped.astype(jnp.float32), axis=0)
    weight_grads = shares.astype(jnp.bfloat16)
    back_grad, back_gate = (
        lax.all_to_all(
            slot_part.reshape(members, capacity, model_width),
            "expert",
            split_axis=0,
            concat_axis=0,
            tiled=True,
        ),
        lax.all_to_all(
            gate_part.reshape(members, capacity), "expert", split_axis=0, concat_axis=0, tiled=True
        ),
    )
    tiled = jnp.broadcast_to(
        place_bf.reshape(experts, 1, capacity, tok_rows), (experts, GROUP, capacity, tok_rows)
    )
    tiled = tiled.reshape(members * capacity, tok_rows)
    grad_tokens = lax.dot_general(
        tiled,
        back_grad.reshape(members * capacity, model_width),
        contract_rows,
        preferred_element_type=jnp.float32,
    ).astype(jnp.bfloat16)
    gate_sum = jnp.sum(
        back_gate.reshape(experts, GROUP, capacity).astype(jnp.float32), axis=1
    ).reshape(slot_count)
    grad_gates = jnp.where(slot_ids >= 0, jnp.take(gate_sum, jnp.maximum(slot_ids, 0), axis=0), 0.0)
    return (
        grad_tokens,
        grad_gates,
        weight_grads[None, :, 0, :],
        weight_grads[None, :, 1, :],
        weight_grads[None, :, 2, :],
    )


def solution(mesh):
    in_specs = (
        P(("expert", "dp"), None),
        P(("expert", "dp"), None),
        P(("expert", "dp"), None),
        P(("expert", "dp"), None),
        P("expert", "dp", None),
        P("expert", "dp", None),
        P("expert", "dp", None),
    )
    out_specs = (
        P(("expert", "dp"), None),
        P(("expert", "dp"), None),
        P("expert", "dp", None),
        P("expert", "dp", None),
        P("expert", "dp", None),
    )
    return jax.shard_map(
        per_device, mesh=mesh, in_specs=in_specs, out_specs=out_specs, check_vma=False
    )
```

profile of v0, /device:TPU:105, one launch (start us, length us, event | category | flops | bytes accessed | tf_op | source)
XLA Modules:
  0.0 467.6 jit_solution(2741525155790413076)
XLA Ops:
  0.6 0.0 copy-start
  0.6 0.7 convert_element_type.116
  1.4 0.7 convert_reduce_fusion
  2.1 0.1 copy.59
  2.2 0.2 reduce_window_sum.11
  2.4 0.7 select_reduce_fusion.1
  3.1 1.2 broadcast_maximum_fusion
  4.4 0.1 select_reduce_fusion
  4.5 0.1 convert_element_type.118
  4.6 0.6 copy.62
  5.2 14.4 %all-to-all-start = ((bf16[32,1,16]{2,1,0:T(2,128)(2,1)}), bf16[32,1,16]{2,1,0:T(2,128)(2,1)S(1)}, u32[]{:S(2)}, u32[]{:S(2)}) async-start(bf16[32,1,16]{2,1,0:T(2,128)(2,1)} %copy.62), calls=%async_computation | async-start | bytes 32768 | tf_op jit(solution)/shard_map/all_to_all | solution.py:74
  19.6 0.3 convolution_convert_fusion.4
  20.0 4.9 %all-to-all-done = bf16[32,1,16]{2,1,0:T(2,128)(2,1)S(1)} async-done(((bf16[32,1,16]{2,1,0:T(2,128)(2,1)}), bf16[32,1,16]{2,1,0:T(2,128)(2,1)S(1)}, u32[]{:S(2)}, u32[]{:S(2)}) %all-to-all-start) | async-done | bytes 1056 | tf_op jit(solution)/shard_map/all_to_all | solution.py:74
  24.9 1.8 broadcast_in_dim.81
  26.7 9.7 %all-to-all-start.2 = ((bf16[32,16,2560]{2,1,0:T(8,128)(2,1)}), bf16[32,16,2560]{2,1,0:T(8,128)(2,1)S(1)}, u32[]{:S(2)}, u32[]{:S(2)}) async-start(bf16[32,16,2560]{2,1,0:T(8,128)(2,1)} %bitcast.108), calls=%async_computation.2 | async-start | bytes 5242880 | tf_op jit(solution)/shard_map/all_to_all | solution.py:64
  36.4 2.3 convolution_convert_fusion.5
  38.7 61.4 %all-to-all-done.2 = bf16[32,16,2560]{2,1,0:T(8,128)(2,1)S(1)} async-done(((bf16[32,16,2560]{2,1,0:T(8,128)(2,1)}), bf16[32,16,2560]{2,1,0:T(8,128)(2,1)S(1)}, u32[]{:S(2)}, u32[]{:S(2)}) %all-to-all-start.2) | async-done | bytes 2621472 | tf_op jit(solution)/shard_map/all_to_all | solution.py:64
  100.0 2.9 broadcast_in_dim.79
  102.9 18.5 %all-to-all-start.1 = ((bf16[32,16,2560]{2,1,0:T(8,128)(2,1)}), bf16[32,16,2560]{2,1,0:T(8,128)(2,1)}, u32[]{:S(2)}, u32[]{:S(2)}) async-start(bf16[32,16,2560]{2,1,0:T(8,128)(2,1)} %bitcast.107), calls=%async_computation.1 | async-start | bytes 5242880 | tf_op jit(solution)/shard_map/all_to_all | solution.py:67
  121.5 0.1 copy.65
  121.6 0.1 copy.64
  121.7 0.1 copy.63
  121.8 83.1 %all_gather.9 = bf16[1,192,2560]{2,0,1:T(2,128)(2,1)} all-gather(bf16[1,12,2560]{2,0,1:T(2,128)(2,1)S(1)} %copy.63), channel_id=1, replica_groups=mesh['expert'=32,'dp'=16] {'dp'}, dimensions={1}, use_global_device_ids=true | all-gather | bytes 1044480 | tf_op jit(solution)/shard_map/all_gather | solution.py:89
  204.9 30.5 %all_gather.10 = bf16[1,192,2560]{2,0,1:T(2,128)(2,1)S(1)} all-gather(bf16[1,12,2560]{2,0,1:T(2,128)(2,1)S(1)} %copy.64), channel_id=1, replica_groups=mesh['expert'=32,'dp'=16] {'dp'}, dimensions={1}, use_global_device_ids=true | all-gather | bytes 1044480 | tf_op jit(solution)/shard_map/all_gather | solution.py:88
  235.4 30.0 %all_gather.11 = bf16[1,192,2560]{2,0,1:T(2,128)(2,1)} all-gather(bf16[1,12,2560]{2,0,1:T(2,128)(2,1)S(1)} %copy.65), channel_id=1, replica_groups=mesh['expert'=32,'dp'=16] {'dp'}, dimensions={1}, use_global_device_ids=true | all-gather | bytes 1044480 | tf_op jit(solution)/shard_map/all_gather | solution.py:87
  265.4 1.8 fusion.9
  267.2 0.0 all-to-all-done.1
  267.2 2.4 multiply_convert_fusion
  269.6 0.0 copy-start.9
  269.6 1.0 fusion.12
  270.6 0.5 copy-done.1
  271.1 1.0 copy-done.3
  272.1 0.0 copy-done.9
  272.1 1.9 fusion.19
  274.1 3.3 fusion.4
  277.4 2.7 fusion
  280.1 0.7 convert_element_type.144
  280.9 24.3 %all-to-all-start.4 = ((bf16[32,1,16]{2,1,0:T(2,128)(2,1)}), bf16[32,1,16]{2,1,0:T(2,128)(2,1)S(1)}, u32[]{:S(2)}, u32[]{:S(2)}) async-start(bf16[32,1,16]{2,1,0:T(2,128)(2,1)} %convert_element_type.144), calls=%async_computation.4 | async-start | bytes 32768 | tf_op jit(solution)/shard_map/all_to_all | solution.py:119
  305.1 5.8 %add_convert_fusion = bf16[512,2560]{1,0:T(8,128)(2,1)} fusion(f32[512,2560]{1,0:T(8,128)} %fusion.4, bf16[1,192,2560]{2,0,1:T(2,128)(2,1)} %copy-done.4, f32[512,192]{0,1:T(8,128)} %copy-done.6, f32[512,192]{0,1:T(8,128)} %copy-done.7), kind=kOutput, calls=%fused_computation.3 | convolution fusion | flops 506527744 | bytes 9633792 | tf_op jit(solution)/shard_map/dot_general | solution.py:35
  310.9 0.0 all-to-all-done.4
  310.9 0.6 copy-done.13
  311.5 11.7 %all-to-all-start.3 = ((bf16[32,16,2560]{2,1,0:T(8,128)(2,1)}), bf16[32,16,2560]{2,1,0:T(8,128)(2,1)}, u32[]{:S(2)}, u32[]{:S(2)}) async-start(bf16[32,16,2560]{2,1,0:T(8,128)(2,1)} %bitcast.104), calls=%async_computation.3 | async-start | bytes 5242880 | tf_op jit(solution)/shard_map/all_to_all | solution.py:112
  323.2 0.8 dot_general.66
  324.0 1.0 dot_general.72
  324.9 1.7 dot_general.69
  326.6 1.7 fusion.2
  328.3 0.7 fusion.1
  329.1 1.0 copy-done.2
  330.1 0.7 fusion.3
  330.8 0.3 pad_maximum_fusion
  331.1 3.6 copy.72
  334.8 54.7 %all-to-all-done.3 = bf16[32,16,2560]{2,1,0:T(8,128)(2,1)} async-done(((bf16[32,16,2560]{2,1,0:T(8,128)(2,1)}), bf16[32,16,2560]{2,1,0:T(8,128)(2,1)}, u32[]{:S(2)}, u32[]{:S(2)}) %all-to-all-start.3) | async-done | bytes 2621472 | tf_op jit(solution)/shard_map/all_to_all | solution.py:112
  389.4 28.3 %all-to-all-start.5 = ((bf16[16,12,3,2560]{3,1,2,0:T(8,128)(2,1)}), bf16[16,12,3,2560]{3,1,2,0:T(8,128)(2,1)}, u32[]{:S(2)}, u32[]{:S(2)}) async-start(bf16[16,12,3,2560]{3,1,2,0:T(8,128)(2,1)} %copy.72), calls=%async_computation.5 | async-start | bytes 7864320 | tf_op jit(solution)/shard_map/all_to_all | solution.py:108
  417.7 0.1 copy.67
  417.8 0.1 reshape.153
  418.1 0.1 reshape.146
  418.1 1.9 gather_fusion
  420.0 0.1 reshape.152
  420.2 0.1 copy.68
  420.2 0.6 compare_select_fusion.1
  420.8 3.1 convolution_convert_fusion.3
  423.9 40.1 %all-to-all-done.5 = bf16[16,12,3,2560]{3,1,2,0:T(8,128)(2,1)} async-done(((bf16[16,12,3,2560]{3,1,2,0:T(8,128)(2,1)}), bf16[16,12,3,2560]{3,1,2,0:T(8,128)(2,1)}, u32[]{:S(2)}, u32[]{:S(2)}) %all-to-all-start.5) | async-done | bytes 2949152 | tf_op jit(solution)/shard_map/all_to_all | solution.py:108
  464.1 2.9 reduce_sum.62
  466.9 0.7 slice_bitcast_fusion
  (39 shorter events, 0.2 us)
Async XLA Ops:
  0.6 19.0 %copy-start = (bf16[128,2560]{1,0:T(8,128)(2,1)S(1)}, bf16[128,2560]{1,0:T(8,128)(2,1)}, u32[]{:S(2)}) copy-start(bf16[128,2560]{1,0:T(8,128)(2,1)} %param.7) | copy-start | bytes 1966084
  4.4 15.2 %copy-start.15 = (s32[128,2]{0,1:T(2,128)}, s32[128,2]{0,1:T(2,128)S(1)}, u32[]{:S(2)}) copy-start(s32[128,2]{0,1:T(2,128)S(1)} %get-tuple-element.21) | copy-start | bytes 3076
  5.2 19.7 %all-to-all-start = ((bf16[32,1,16]{2,1,0:T(2,128)(2,1)}), bf16[32,1,16]{2,1,0:T(2,128)(2,1)S(1)}, u32[]{:S(2)}, u32[]{:S(2)}) async-start(bf16[32,1,16]{2,1,0:T(2,128)(2,1)} %copy.62), calls=%async_computation | async-start | bytes 32768 | tf_op jit(solution)/shard_map/all_to_all | solution.py:74
  26.7 73.3 %all-to-all-start.2 = ((bf16[32,16,2560]{2,1,0:T(8,128)(2,1)}), bf16[32,16,2560]{2,1,0:T(8,128)(2,1)S(1)}, u32[]{:S(2)}, u32[]{:S(2)}) async-start(bf16[32,16,2560]{2,1,0:T(8,128)(2,1)} %bitcast.108), calls=%async_computation.2 | async-start | bytes 5242880 | tf_op jit(solution)/shard_map/all_to_all | solution.py:64
  102.9 18.6 %copy-start.10 = (bf16[1,12,2560]{2,1,0:T(8,128)(2,1)S(1)}, bf16[1,12,2560]{2,1,0:T(8,128)(2,1)}, u32[]{:S(2)}) copy-start(bf16[1,12,2560]{2,1,0:T(8,128)(2,1)} %param.11) | copy-start | bytes 184324
  102.9 18.7 %copy-start.11 = (bf16[1,12,2560]{2,1,0:T(8,128)(2,1)S(1)}, bf16[1,12,2560]{2,1,0:T(8,128)(2,1)}, u32[]{:S(2)}) copy-start(bf16[1,12,2560]{2,1,0:T(8,128)(2,1)} %param.12) | copy-start | bytes 184324
  102.9 18.8 %copy-start.12 = (bf16[1,12,2560]{2,1,0:T(8,128)(2,1)S(1)}, bf16[1,12,2560]{2,1,0:T(8,128)(2,1)}, u32[]{:S(2)}) copy-start(bf16[1,12,2560]{2,1,0:T(8,128)(2,1)} %param.13) | copy-start | bytes 184324
  102.9 164.3 %all-to-all-start.1 = ((bf16[32,16,2560]{2,1,0:T(8,128)(2,1)}), bf16[32,16,2560]{2,1,0:T(8,128)(2,1)}, u32[]{:S(2)}, u32[]{:S(2)}) async-start(bf16[32,16,2560]{2,1,0:T(8,128)(2,1)} %bitcast.107), calls=%async_computation.1 | async-start | bytes 5242880 | tf_op jit(solution)/shard_map/all_to_all | solution.py:67
  235.4 30.0 %copy-start.4 = (bf16[1,192,2560]{2,0,1:T(2,128)(2,1)}, bf16[1,192,2560]{2,0,1:T(2,128)(2,1)S(1)}, u32[]{:S(2)}) copy-start(bf16[1,192,2560]{2,0,1:T(2,128)(2,1)S(1)} %all_gather.10) | copy-start | bytes 2949124
  267.2 2.4 copy-start.5
  269.6 1.5 copy-start.1
  269.6 2.5 copy-start.3
  269.6 2.5 copy-start.9
  272.1 1.9 copy-start.6
  274.1 3.3 copy-start.7
  280.9 30.0 %all-to-all-start.4 = ((bf16[32,1,16]{2,1,0:T(2,128)(2,1)}), bf16[32,1,16]{2,1,0:T(2,128)(2,1)S(1)}, u32[]{:S(2)}, u32[]{:S(2)}) async-start(bf16[32,1,16]{2,1,0:T(2,128)(2,1)} %convert_element_type.144), calls=%async_computation.4 | async-start | bytes 32768 | tf_op jit(solution)/shard_map/all_to_all | solution.py:119
  310.9 0.6 copy-start.13
  311.5 77.9 %all-to-all-start.3 = ((bf16[32,16,2560]{2,1,0:T(8,128)(2,1)}), bf16[32,16,2560]{2,1,0:T(8,128)(2,1)}, u32[]{:S(2)}, u32[]{:S(2)}) async-start(bf16[32,16,2560]{2,1,0:T(8,128)(2,1)} %bitcast.104), calls=%async_computation.3 | async-start | bytes 5242880 | tf_op jit(solution)/shard_map/all_to_all | solution.py:112
  326.6 1.7 copy-start.8
  328.3 1.7 copy-start.2
  334.8 83.0 %copy-start.17 = (s32[128,2]{0,1:T(2,128)S(1)}, s32[128,2]{0,1:T(2,128)}, u32[]{:S(2)}) copy-start(s32[128,2]{0,1:T(2,128)} %get-tuple-element.20) | copy-start | bytes 3076
  334.8 83.2 %copy-start.14 = (bf16[32,1,16]{2,1,0:T(2,128)(2,1)S(1)}, bf16[32,1,16]{2,1,0:T(2,128)(2,1)}, u32[]{:S(2)}) copy-start(bf16[32,1,16]{2,1,0:T(2,128)(2,1)} %copy-done.13) | copy-start | bytes 3076
  389.4 74.7 %all-to-all-start.5 = ((bf16[16,12,3,2560]{3,1,2,0:T(8,128)(2,1)}), bf16[16,12,3,2560]{3,1,2,0:T(8,128)(2,1)}, u32[]{:S(2)}, u32[]{:S(2)}) async-start(bf16[16,12,3,2560]{3,1,2,0:T(8,128)(2,1)} %copy.72), calls=%async_computation.5 | async-start | bytes 7864320 | tf_op jit(solution)/shard_map/all_to_all | solution.py:108
  418.1 2.1 copy-start.16
where the time goes:
time: 469 us; the launch traced here: 468 us
  waiting for transfers between devices  161 us (34%)
  blocking collectives  144 us (31%)
  starting transfers between devices  107 us (23%)
  matrix products  25.3 us (5%)
  local copies, waits for them, and re-layouts  19.9 us (4%)
  other arithmetic  9.89 us (2%)
    all_gather x1, blocking collectives, per_device(): lax.all_gather(down_proj, 'dp', axis=1, tiled=True)  83.1 us
    all_to_all x1, waiting for transfers between devices, per_device(): lax.all_to_all(spread_out(sent_x, experts, capacity), 'expert', split_axi...  61.4 us
    all_to_all x1, waiting for transfers between devices, per_device(): lax.all_to_all(slot_part.reshape(members, capacity, model_width), 'expert...  54.7 us
    all_to_all x1, waiting for transfers between devices, per_device(): lax.all_to_all(parted, 'dp', split_axis=0, concat_axis=0, tiled=True)  40.1 us
    all_gather x1, blocking collectives, per_device(): lax.all_gather(up_proj, 'dp', axis=1, tiled=True)  30.5 us
    all_gather x1, blocking collectives, per_device(): lax.all_gather(gate_proj, 'dp', axis=1, tiled=True)  30 us
    all_to_all x1, starting transfers between devices, per_device(): lax.all_to_all(parted, 'dp', split_axis=0, concat_axis=0, tiled=True)  28.3 us
    all_to_all x1, starting transfers between devices, per_device(): lax.all_to_all(gate_part.reshape(members, capacity), 'expert', split_axis...  24.3 us
  transfers between devices with their start and end apart: 6, of which 4 were waited for; matrix products, arithmetic and copies ran while one was open for 6% of the time, Pallas kernels for 0%

commit v1 on v0

--- a/solution.py
+++ b/solution.py
@@ -4,6 +4,9 @@
 from jax.sharding import PartitionSpec as P
 
 GROUP = 4
+extend_sections = lambda x0: jnp.concatenate(
+    lax.all_to_all(jnp.stack([x0] * lax.axis_size("dp"), axis=0), "dp", 0, 0), axis=1
+)
 
 
 def slot_tables(route_block, experts, capacity):
@@ -84,7 +87,7 @@
     rows_gate = got_gate.reshape(-1).astype(jnp.float32)
     scaled_dy = (rows_gate[:, None] * rows_dy.astype(jnp.float32)).astype(jnp.bfloat16)
     full_gate, full_up, full_down = (
-        lax.all_gather(gate_proj, "dp", axis=1, tiled=True),
+        extend_sections(gate_proj),
         lax.all_gather(up_proj, "dp", axis=1, tiled=True),
         lax.all_gather(down_proj, "dp", axis=1, tiled=True),
     )

time: 469 us -> 494 us (1.053)
  the two profiles are of different devices: /device:TPU:105 before, /device:TPU:121 now
where the time goes in v1:
time: 494 us; the launch traced here: 493 us
  waiting for transfers between devices  204 us (41%)
  blocking collectives  150 us (30%)
  starting transfers between devices  78.1 us (16%)
  matrix products  26.9 us (5%)
  local copies, waits for them, and re-layouts  23.2 us (5%)
  other arithmetic  9.89 us (2%)
    all_gather x1, blocking collectives, per_device(): lax.all_gather(down_proj, 'dp', axis=1, tiled=True)  94.6 us
    all_to_all x1, waiting for transfers between devices, per_device(): lax.all_to_all(slot_part.reshape(members, capacity, model_width), 'expert...  85.8 us
    all_to_all x1, waiting for transfers between devices, per_device(): lax.all_to_all(spread_out(sent_x, experts, capacity), 'expert', split_axi...  60.4 us
    all_to_all x1, waiting for transfers between devices, per_device(): lax.all_to_all(parted, 'dp', split_axis=0, concat_axis=0, tiled=True)  39.2 us
    all_gather x1, blocking collectives, per_device(): lax.all_gather(up_proj, 'dp', axis=1, tiled=True)  34.1 us
    all_to_all x1, starting transfers between devices, per_device(): lax.all_to_all(gate_part.reshape(members, capacity), 'expert', split_axis...  33.7 us
    all_to_all x1, blocking collectives, per_device(): lax.all_to_all(spread_out(sent_gate, experts, capacity), 'expert', split_...  21 us
    all_to_all x1, waiting for transfers between devices, lax.all_to_all(jnp.stack([x0] * lax.axis_size('dp'), axis=0), 'dp', 0, 0)  17.8 us
  transfers between devices with their start and end apart: 6, of which 5 were waited for; matrix products, arithmetic and copies ran while one was open for 6% of the time, Pallas kernels for 0%

profile of v1, /device:TPU:121, one launch (start us, length us, event | category | flops | bytes accessed | tf_op | source)
XLA Modules:
  0.0 493.3 jit_solution(1068791060486408771)
XLA Ops:
  0.6 0.0 copy-start
  0.6 0.7 convert_element_type.116
  1.4 0.7 convert_reduce_fusion
  2.1 0.1 copy.57
  2.2 0.2 reduce_window_sum.11
  2.4 0.7 select_reduce_fusion.1
  3.1 1.2 broadcast_maximum_fusion
  4.4 0.1 select_reduce_fusion
  4.5 0.1 convert_element_type.118
  4.6 21.0 %all_to_all.40 = bf16[32,1,16]{2,1,0:T(2,128)(2,1)S(1)} all-to-all(bf16[32,1,16]{2,1,0:T(2,128)(2,1)S(1)} %copy.60), channel_id=1, replica_groups=mesh['expert'=32,'dp'=16] {'expert'}, dimensions={0} | all-to-all | bytes 2048 | tf_op jit(solution)/shard_map/all_to_all | solution.py:77
  25.6 2.1 stack.4
  27.7 7.5 %all-to-all-start.3 = ((bf16[16,1,12,2560]{3,2,1,0:T(8,128)(2,1)}), bf16[16,1,12,2560]{3,2,1,0:T(8,128)(2,1)S(1)}, u32[]{:S(2)}, u32[]{:S(2)}) async-start(bf16[16,1,12,2560]{3,2,1,0:T(8,128)(2,1)} %stack.4), calls=%async_computation.3 | async-start | bytes 2621440 | tf_op jit(solution)/shard_map/all_to_all | solution.py:8
  35.3 0.3 convolution_convert_fusion.4
  35.6 17.8 %all-to-all-done.3 = bf16[16,1,12,2560]{3,2,1,0:T(8,128)(2,1)S(1)} async-done(((bf16[16,1,12,2560]{3,2,1,0:T(8,128)(2,1)}), bf16[16,1,12,2560]{3,2,1,0:T(8,128)(2,1)S(1)}, u32[]{:S(2)}, u32[]{:S(2)}) %all-to-all-start.3) | async-done | bytes 983072 | tf_op jit(solution)/shard_map/all_to_all | solution.py:8
  53.4 1.9 broadcast_in_dim.81
  55.3 8.1 %all-to-all-start.2 = ((bf16[32,16,2560]{2,1,0:T(8,128)(2,1)}), bf16[32,16,2560]{2,1,0:T(8,128)(2,1)S(1)}, u32[]{:S(2)}, u32[]{:S(2)}) async-start(bf16[32,16,2560]{2,1,0:T(8,128)(2,1)} %bitcast.104), calls=%async_computation.2 | async-start | bytes 5242880 | tf_op jit(solution)/shard_map/all_to_all | solution.py:67
  63.4 2.3 convolution_convert_fusion.5
  65.6 60.4 %all-to-all-done.2 = bf16[32,16,2560]{2,1,0:T(8,128)(2,1)S(1)} async-done(((bf16[32,16,2560]{2,1,0:T(8,128)(2,1)}), bf16[32,16,2560]{2,1,0:T(8,128)(2,1)S(1)}, u32[]{:S(2)}, u32[]{:S(2)}) %all-to-all-start.2) | async-done | bytes 2621472 | tf_op jit(solution)/shard_map/all_to_all | solution.py:67
  126.0 2.9 broadcast_in_dim.79
  129.0 13.8 %all-to-all-start.1 = ((bf16[32,16,2560]{2,1,0:T(8,128)(2,1)}), bf16[32,16,2560]{2,1,0:T(8,128)(2,1)}, u32[]{:S(2)}, u32[]{:S(2)}) async-start(bf16[32,16,2560]{2,1,0:T(8,128)(2,1)} %bitcast.103), calls=%async_computation.1 | async-start | bytes 5242880 | tf_op jit(solution)/shard_map/all_to_all | solution.py:70
  142.8 0.1 copy.62
  142.9 0.1 copy.61
  143.0 94.6 %all_gather.6 = bf16[1,192,2560]{2,0,1:T(2,128)(2,1)} all-gather(bf16[1,12,2560]{2,0,1:T(2,128)(2,1)S(1)} %copy.61), channel_id=1, replica_groups=mesh['expert'=32,'dp'=16] {'dp'}, dimensions={1}, use_global_device_ids=true | all-gather | bytes 1044480 | tf_op jit(solution)/shard_map/all_gather | solution.py:92
  237.7 34.1 %all_gather.7 = bf16[1,192,2560]{2,0,1:T(2,128)(2,1)} all-gather(bf16[1,12,2560]{2,0,1:T(2,128)(2,1)S(1)} %copy.62), channel_id=1, replica_groups=mesh['expert'=32,'dp'=16] {'dp'}, dimensions={1}, use_global_device_ids=true | all-gather | bytes 1044480 | tf_op jit(solution)/shard_map/all_gather | solution.py:91
  271.8 2.2 squeeze_reshape.3
  274.1 3.3 fusion.5
  277.4 0.0 all-to-all-done.1
  277.4 2.4 multiply_convert_fusion
  279.8 0.0 copy-start.8
  279.8 1.0 fusion.8
  280.8 0.4 copy-done.1
  281.2 0.5 copy-done.4
  281.7 0.3 copy-done.8
  282.0 2.0 fusion.15
  284.0 3.3 fusion.24
  287.2 2.7 fusion
  290.0 0.7 convert_element_type.144
  290.7 33.7 %all-to-all-start.5 = ((bf16[32,1,16]{2,1,0:T(2,128)(2,1)}), bf16[32,1,16]{2,1,0:T(2,128)(2,1)S(1)}, u32[]{:S(2)}, u32[]{:S(2)}) async-start(bf16[32,1,16]{2,1,0:T(2,128)(2,1)} %convert_element_type.144), calls=%async_computation.5 | async-start | bytes 32768 | tf_op jit(solution)/shard_map/all_to_all | solution.py:122
  324.4 5.8 %add_convert_fusion = bf16[512,2560]{1,0:T(8,128)(2,1)} fusion(f32[512,2560]{1,0:T(8,128)} %fusion.24, bf16[1,192,2560]{2,0,1:T(2,128)(2,1)} %all_gather.7, f32[512,192]{0,1:T(8,128)} %copy-done.5, f32[512,192]{0,1:T(8,128)} %copy-done.6), kind=kOutput, calls=%fused_computation.3 | convolution fusion | flops 506527744 | bytes 9633792 | tf_op jit(solution)/shard_map/dot_general | solution.py:38
  330.2 1.1 all-to-all-done.5
  331.4 0.6 copy-done.12
  332.0 10.6 %all-to-all-start.4 = ((bf16[32,16,2560]{2,1,0:T(8,128)(2,1)}), bf16[32,16,2560]{2,1,0:T(8,128)(2,1)}, u32[]{:S(2)}, u32[]{:S(2)}) async-start(bf16[32,16,2560]{2,1,0:T(8,128)(2,1)} %bitcast.100), calls=%async_computation.4 | async-start | bytes 5242880 | tf_op jit(solution)/shard_map/all_to_all | solution.py:115
  342.6 0.7 dot_general.66
  343.3 1.0 dot_general.72
  344.3 1.7 dot_general.69
  345.9 1.7 fusion.2
  347.7 0.7 fusion.1
  348.4 1.0 copy-done.2
  349.4 0.7 fusion.3
  350.1 0.3 pad_maximum_fusion
  350.4 3.5 copy.69
  354.0 85.8 %all-to-all-done.4 = bf16[32,16,2560]{2,1,0:T(8,128)(2,1)} async-done(((bf16[32,16,2560]{2,1,0:T(8,128)(2,1)}), bf16[32,16,2560]{2,1,0:T(8,128)(2,1)}, u32[]{:S(2)}, u32[]{:S(2)}) %all-to-all-start.4) | async-done | bytes 2621472 | tf_op jit(solution)/shard_map/all_to_all | solution.py:115
  439.8 4.4 all-to-all-start.6
  444.3 0.1 copy.64
  444.4 0.1 reshape.156
  444.6 0.1 reshape.149
  444.7 1.9 gather_fusion
  446.6 0.1 reshape.155
  446.7 0.1 copy.65
  446.8 0.6 compare_select_fusion.1
  447.4 3.1 convolution_convert_fusion.3
  450.5 39.2 %all-to-all-done.6 = bf16[16,12,3,2560]{3,1,2,0:T(8,128)(2,1)} async-done(((bf16[16,12,3,2560]{3,1,2,0:T(8,128)(2,1)}), bf16[16,12,3,2560]{3,1,2,0:T(8,128)(2,1)}, u32[]{:S(2)}, u32[]{:S(2)}) %all-to-all-start.6) | async-done | bytes 2949152 | tf_op jit(solution)/shard_map/all_to_all | solution.py:111
  489.7 2.9 reduce_sum.62
  492.6 0.7 slice_bitcast_fusion
  (38 shorter events, 0.2 us)
Async XLA Ops:
  0.6 34.6 %copy-start = (bf16[128,2560]{1,0:T(8,128)(2,1)S(1)}, bf16[128,2560]{1,0:T(8,128)(2,1)}, u32[]{:S(2)}) copy-start(bf16[128,2560]{1,0:T(8,128)(2,1)} %param.7) | copy-start | bytes 1966084
  4.4 31.2 %copy-start.14 = (s32[128,2]{0,1:T(2,128)}, s32[128,2]{0,1:T(2,128)S(1)}, u32[]{:S(2)}) copy-start(s32[128,2]{0,1:T(2,128)S(1)} %get-tuple-element.21) | copy-start | bytes 3076
  27.7 25.7 %all-to-all-start.3 = ((bf16[16,1,12,2560]{3,2,1,0:T(8,128)(2,1)}), bf16[16,1,12,2560]{3,2,1,0:T(8,128)(2,1)S(1)}, u32[]{:S(2)}, u32[]{:S(2)}) async-start(bf16[16,1,12,2560]{3,2,1,0:T(8,128)(2,1)} %stack.4), calls=%async_computation.3 | async-start | bytes 2621440 | tf_op jit(solution)/shard_map/all_to_all | solution.py:8
  53.4 1.9 copy-start.3
  55.3 70.7 %all-to-all-start.2 = ((bf16[32,16,2560]{2,1,0:T(8,128)(2,1)}), bf16[32,16,2560]{2,1,0:T(8,128)(2,1)S(1)}, u32[]{:S(2)}, u32[]{:S(2)}) async-start(bf16[32,16,2560]{2,1,0:T(8,128)(2,1)} %bitcast.104), calls=%async_computation.2 | async-start | bytes 5242880 | tf_op jit(solution)/shard_map/all_to_all | solution.py:67
  129.0 13.8 %copy-start.10 = (bf16[1,12,2560]{2,1,0:T(8,128)(2,1)S(1)}, bf16[1,12,2560]{2,1,0:T(8,128)(2,1)}, u32[]{:S(2)}) copy-start(bf16[1,12,2560]{2,1,0:T(8,128)(2,1)} %param.12) | copy-start | bytes 184324
  129.0 14.0 %copy-start.11 = (bf16[1,12,2560]{2,1,0:T(8,128)(2,1)S(1)}, bf16[1,12,2560]{2,1,0:T(8,128)(2,1)}, u32[]{:S(2)}) copy-start(bf16[1,12,2560]{2,1,0:T(8,128)(2,1)} %param.13) | copy-start | bytes 184324
  129.0 148.4 %all-to-all-start.1 = ((bf16[32,16,2560]{2,1,0:T(8,128)(2,1)}), bf16[32,16,2560]{2,1,0:T(8,128)(2,1)}, u32[]{:S(2)}, u32[]{:S(2)}) async-start(bf16[32,16,2560]{2,1,0:T(8,128)(2,1)} %bitcast.103), calls=%async_computation.1 | async-start | bytes 5242880 | tf_op jit(solution)/shard_map/all_to_all | solution.py:70
  277.4 2.4 copy-start.7
  279.8 1.5 copy-start.1
  279.8 1.9 copy-start.4
  279.8 2.2 copy-start.8
  282.0 2.0 copy-start.5
  284.0 3.3 copy-start.6
  290.7 40.7 %all-to-all-start.5 = ((bf16[32,1,16]{2,1,0:T(2,128)(2,1)}), bf16[32,1,16]{2,1,0:T(2,128)(2,1)S(1)}, u32[]{:S(2)}, u32[]{:S(2)}) async-start(bf16[32,1,16]{2,1,0:T(2,128)(2,1)} %convert_element_type.144), calls=%async_computation.5 | async-start | bytes 32768 | tf_op jit(solution)/shard_map/all_to_all | solution.py:122
  331.4 0.6 copy-start.12
  332.0 107.8 %all-to-all-start.4 = ((bf16[32,16,2560]{2,1,0:T(8,128)(2,1)}), bf16[32,16,2560]{2,1,0:T(8,128)(2,1)}, u32[]{:S(2)}, u32[]{:S(2)}) async-start(bf16[32,16,2560]{2,1,0:T(8,128)(2,1)} %bitcast.100), calls=%async_computation.4 | async-start | bytes 5242880 | tf_op jit(solution)/shard_map/all_to_all | solution.py:115
  345.9 1.7 copy-start.9
  347.7 1.7 copy-start.2
  354.0 90.3 %copy-start.16 = (s32[128,2]{0,1:T(2,128)S(1)}, s32[128,2]{0,1:T(2,128)}, u32[]{:S(2)}) copy-start(s32[128,2]{0,1:T(2,128)} %get-tuple-element.20) | copy-start | bytes 3076
  354.0 90.6 %copy-start.13 = (bf16[32,1,16]{2,1,0:T(2,128)(2,1)S(1)}, bf16[32,1,16]{2,1,0:T(2,128)(2,1)}, u32[]{:S(2)}) copy-start(bf16[32,1,16]{2,1,0:T(2,128)(2,1)} %copy-done.12) | copy-start | bytes 3076
  439.8 49.9 %all-to-all-start.6 = ((bf16[16,12,3,2560]{3,1,2,0:T(8,128)(2,1)}), bf16[16,12,3,2560]{3,1,2,0:T(8,128)(2,1)}, u32[]{:S(2)}, u32[]{:S(2)}) async-start(bf16[16,12,3,2560]{3,1,2,0:T(8,128)(2,1)} %copy.69), calls=%async_computation.6 | async-start | bytes 7864320 | tf_op jit(solution)/shard_map/all_to_all | solution.py:111
  444.7 2.1 copy-start.15
